TPU v7x, 128 devices: a whole 4x4x4 slice. The times are simulated.
128 devices in a mesh: kpt: 8 (over z, core), row: 4 (over y), col: 4 (over x).
Axes of the slice: x: 4, y: 4, z: 4, core: 2. Of those that a mesh axis runs over, the one named last changes fastest.
Arguments:
- cycle_amplitudes: float32 [16, 2, 1024, 2048], P('kpt', None, 'row', 'col'), may hold values from -6 to 6
- cycle_integrals: float32 [16, 2, 2048, 2048], P('kpt', None, 'row', 'col'), may hold values from -0.09375 to 0.09375
- ladder_weight: float32 [16, 2, 1024, 1024], P('kpt', None, ('row', 'col')), may hold values from -0.125 to 0.125
- momentum_table: int32 [16, 16, 16], replicated, may hold values from 0 to 15, as said below
- transfer_slots: int32 [16], replicated, may hold values from 0 to 15, each once
- momentum_slots: int32 [16], replicated, may hold values from 0 to 15, each once
Outputs:
- residual: float32 [16, 2, 1024, 2048], P('kpt', None, 'row', 'col')
Inputs may be any that keep to these rules, and one draw needn't show every extreme that they name: momentum_table[a, b, c] is the label of a + b - c on a periodic grid of 16 k-points; the labels form an abelian group under this addition with label 0 as its anchor. `transfer_slots`: every momentum transfer stands in exactly one slot. `momentum_slots`: every total momentum stands in exactly one slot.
All inputs are finite; a program needn't handle non-finite values.
Results may differ from a plain program's by a relative error of at most 0.00007.
Values sent between devices are 32-bit elements; how exact they have to be, the bound alone decides.
A program may use at most 192 MiB of HBM per device.

v0:
```python
import jax
import jax.numpy as jnp
from jax import lax
from jax.sharding import PartitionSpec as P

NK = 16


PRECISE = lax.Precision.HIGHEST


def complex_product(left_op, right_op):

    def multiply(first_mat, second_mat):
        return jnp.einsum(
            "qmk,qkn->qmn",
            first_mat,
            second_mat,
            precision=PRECISE,
            preferred_element_type=jnp.float32,
        )

    left_real, left_imag = (left_op[:, 0], left_op[:, 1])
    right_real, right_imag = (right_op[:, 0], right_op[:, 1])
    real_part = multiply(left_real, right_real) - multiply(left_imag, right_imag)
    imag_part = multiply(left_real, right_imag) + multiply(left_imag, right_real)
    return jnp.stack([real_part, imag_part], axis=1)


def table_lookup(lookup_table, first_label, second_label):
    label_count = lookup_table.shape[0]
    labels = jnp.arange(label_count, dtype=jnp.int32)
    one_first = (first_label[..., None] == labels).astype(jnp.int32)
    one_second = (second_label[..., None] == labels).astype(jnp.int32)
    return jnp.sum(one_first[..., :, None] * one_second[..., None, :] * lookup_table, axis=(-2, -1))


def select_kpoint(add_table, sub_table, momenta, transfers, kpoints):
    return table_lookup(sub_table, momenta, table_lookup(add_table, transfers, kpoints))


def body(
    cycle_amplitudes, cycle_integrals, ladder_weight, momentum_table, transfer_slots, momentum_slots
):
    kpt_count = lax.axis_size("kpt")
    row_count = lax.axis_size("row")
    slot_count = cycle_amplitudes.shape[0]
    kpoint_count = NK
    row_kpoints = kpoint_count // row_count
    row_pairs = cycle_amplitudes.shape[2] // row_kpoints
    col_pairs = cycle_integrals.shape[3] // kpoint_count
    add_table = momentum_table[:, :, 0]
    sub_table = momentum_table[:, 0, :]
    own_kpt = lax.axis_index("kpt")
    own_row = lax.axis_index("row")
    own_transfers = lax.dynamic_slice_in_dim(transfer_slots, own_kpt * slot_count, slot_count)
    own_momenta = lax.dynamic_slice_in_dim(momentum_slots, own_kpt * slot_count, slot_count)
    all_transfers = transfer_slots.reshape(kpt_count, slot_count)
    all_momenta = momentum_slots.reshape(kpt_count, slot_count)
    own_kpoints = own_row * row_kpoints + jnp.arange(row_kpoints, dtype=jnp.int32)
    labels = jnp.arange(kpoint_count, dtype=jnp.int32)
    whole_amp = lax.all_gather(cycle_amplitudes, "col", axis=3, tiled=True)
    cycle_out = complex_product(
        whole_amp, lax.all_gather(cycle_integrals, "row", axis=2, tiled=True)
    )
    source_kb = select_kpoint(
        add_table,
        sub_table,
        all_momenta[None, None, :, :],
        own_transfers[:, None, None, None],
        own_kpoints[None, :, None, None],
    )
    source_select = (source_kb[:, :, None, :, :] == labels[None, None, :, None, None]).astype(
        jnp.float32
    )
    sub_pairs = col_pairs // row_count
    blocks = cycle_out.reshape(
        slot_count, 2, row_kpoints, row_pairs, row_count, sub_pairs, kpoint_count
    )
    outgoing = jnp.einsum("qctpxjk,qtkam->axmqctpj", blocks, source_select, precision=PRECISE)
    outgoing = outgoing.reshape(
        kpt_count * row_count, slot_count, slot_count, 2, row_kpoints, row_pairs * sub_pairs
    )
    incoming = lax.all_to_all(outgoing, ("kpt", "row"), split_axis=0, concat_axis=0, tiled=True)
    incoming = incoming.reshape(
        kpt_count, row_count, slot_count, slot_count, 2, row_kpoints, row_pairs, sub_pairs
    )
    every_kpoint = (
        jnp.arange(row_count, dtype=jnp.int32)[:, None] * row_kpoints
        + jnp.arange(row_kpoints, dtype=jnp.int32)[None, :]
    )
    target_kb = select_kpoint(
        add_table,
        sub_table,
        own_momenta[None, None, :, None, None],
        all_transfers[:, :, None, None, None],
        every_kpoint[None, None, None, :, :],
    )
    target_select = (target_kb[..., None] == labels).astype(jnp.float32)
    grouped = jnp.einsum("axmqctpj,aqmxtk->mcxtpjk", incoming, target_select, precision=PRECISE)
    grouped = grouped.reshape(slot_count, 2, kpoint_count * row_pairs, sub_pairs * kpoint_count)
    ladder_out = complex_product(
        lax.all_gather(ladder_weight, ("row", "col"), axis=2, tiled=True), grouped
    )
    ladder_out = ladder_out.reshape(
        slot_count, 2, row_count, row_kpoints, row_pairs, sub_pairs, kpoint_count
    )
    sent_back = jnp.einsum("mcxtpjk,aqmxtk->axmqctpj", ladder_out, target_select, precision=PRECISE)
    sent_back = sent_back.reshape(
        kpt_count * row_count, slot_count, slot_count, 2, row_kpoints, row_pairs * sub_pairs
    )
    returned = lax.all_to_all(sent_back, ("kpt", "row"), split_axis=0, concat_axis=0, tiled=True)
    returned = returned.reshape(
        kpt_count, row_count, slot_count, slot_count, 2, row_kpoints, row_pairs, sub_pairs
    )
    ladder_part = jnp.einsum("axmqctpj,qtkam->qctpxjk", returned, source_select, precision=PRECISE)
    return cycle_out + ladder_part.reshape(cycle_out.shape)


def solution(mesh):
    return jax.shard_map(
        body,
        mesh=mesh,
        in_specs=(
            P("kpt", None, "row", "col"),
            P("kpt", None, "row", "col"),
            P("kpt", None, ("row", "col"), None),
            P(),
            P(),
            P(),
        ),
        out_specs=P("kpt", None, "row", "col"),
        check_vma=False,
    )
```

profile of v0, /device:TPU:9, one launch (start us, length us, event | category | flops | bytes accessed | tf_op | source)
XLA Modules:
  0.0 652.9 jit_solution(12091052795312436988)
XLA Ops:
  6.5 3.1 copy.63
  9.7 4.6 copy.64
  14.4 1.1 copy-done.5
  15.5 1.0 copy.79
  17.5 2.4 multiply_reduce_fusion.2
  20.1 75.1 %all-gather.4.cloned.1.call-done = f32[2,2,256,2048]{3,2,0,1:T(8,128)} async-done(((f32[2,2,256,512]{3,2,0,1:T(8,128)}), f32[2,2,256,2048]{3,2,0,1:T(8,128)}) %all-gather.4.cloned.1.call-update) | async-done | bytes 8388624 | tf_op jit(solution)/shard_map/all_gather | solution.py:62
  95.2 156.8 %all-gather.6.cloned.1.call-done = f32[2,2,2048,512]{3,2,0,1:T(8,128)} async-done(((f32[2,2,512,512]{3,2,0,1:T(8,128)}), f32[2,2,2048,512]{3,2,0,1:T(8,128)}) %all-gather.6.cloned.1.call-update) | async-done | bytes 16777232 | tf_op jit(solution)/shard_map/all_gather | solution.py:64
  251.9 10.9 %fusion.1 = f32[2,256,512]{2,1,0:T(8,128)S(1)} fusion(f32[2,2,2048,512]{3,2,0,1:T(8,128)} %all-gather.6.cloned.1.call-done, f32[2,2,256,2048]{3,2,0,1:T(8,128)} %all-gather.4.cloned.1.call-done), kind=kOutput, calls=%fused_computation.5 | convolution fusion | flops 6442450944 | bytes 13631488 | tf_op jit(solution)/shard_map/qmk,qkn->qmn/dot_general | solution.py:15
  262.8 9.8 %fusion.20 = f32[2,256,512]{2,1,0:T(8,128)S(1)} fusion(f32[2,256,512]{2,1,0:T(8,128)S(1)} %fusion.1, f32[2,2,2048,512]{3,2,0,1:T(8,128)} %all-gather.6.cloned.1.call-done, f32[2,2,256,2048]{3,2,0,1:T(8,128)S(1)} %copy-done), kind=kOutput, calls=%fused_computation.33 | convolution fusion | flops 6442713088 | bytes 14680064 | tf_op jit(solution)/shard_map/qmk,qkn->qmn/dot_general | solution.py:15
  272.6 1.3 copy.68
  273.9 2.1 stack.27
  276.0 1.6 copy.70
  277.6 10.8 %fusion = f32[2,256,512]{2,1,0:T(8,128)S(1)} fusion(f32[2,2,2048,512]{3,2,0,1:T(8,128)} %all-gather.6.cloned.1.call-done, f32[2,2,256,2048]{3,2,0,1:T(8,128)} %all-gather.4.cloned.1.call-done), kind=kOutput, calls=%fused_computation.4 | convolution fusion | flops 6442450944 | bytes 13631488 | tf_op jit(solution)/shard_map/qmk,qkn->qmn/dot_general | solution.py:15
  288.4 9.8 %fusion.21 = f32[2,256,512]{2,1,0:T(8,128)S(1)} fusion(f32[2,256,512]{2,1,0:T(8,128)S(1)} %fusion, f32[2,2,2048,512]{3,2,0,1:T(8,128)} %all-gather.6.cloned.1.call-done, f32[2,2,256,2048]{3,2,0,1:T(8,128)S(1)} %bitcast.122), kind=kOutput, calls=%fused_computation.34 | convolution fusion | flops 6442713088 | bytes 14680064 | tf_op jit(solution)/shard_map/qmk,qkn->qmn/dot_general | solution.py:15
  298.6 2.2 stack.28
  300.8 2.0 copy.71
  303.0 4.3 fusion.15
  307.4 18.1 %copy.100 = f32[8,4,2,2,2,4,64,8]{7,6,5,4,3,2,1,0:T(8,128)} copy(f32[8,4,2,2,2,4,64,8]{6,0,7,1,4,2,5,3:T(8,128)} %fusion.15) | data formatting | bytes 4194304 | tf_op jit(solution)/shard_map/reshape | solution.py:81
  325.4 25.3 %reshape.232 = f32[32,2,2,2,4,512]{5,4,3,2,1,0:T(4,128)} reshape(f32[8,4,2,2,2,4,64,8]{7,6,5,4,3,2,1,0:T(8,128)} %copy.100) | data formatting | bytes 4194304 | tf_op jit(solution)/shard_map/reshape | solution.py:81
  350.7 7.9 %all-to-all-start = ((f32[32,2,2,2,4,512]{5,4,3,2,1,0:T(4,128)}), f32[32,2,2,2,4,512]{5,4,3,2,1,0:T(4,128)S(1)}, u32[]{:S(2)}, u32[]{:S(2)}) async-start(f32[32,2,2,2,4,512]{5,4,3,2,1,0:T(4,128)} %reshape.232), calls=%async_computation | async-start | bytes 4194304 | tf_op jit(solution)/shard_map/all_to_all | solution.py:84
  359.0 4.9 multiply_reduce_fusion.1
  364.1 9.4 %multiply_reduce_fusion = s32[8,2,2,4,4]{4,3,2,1,0:T(4,128)S(1)} fusion(s32[16,16]{1,0:T(8,128)S(1)} %bitcast.129, s32[8,2,4,4,16]{4,3,2,1,0:T(4,128)S(1)} %fusion.27, s32[2,16]{1,0:T(2,128)S(1)} %compare_convert_fusion.2), kind=kLoop, calls=%fused_computation.22 | loop fusion | flops 392704 | bytes 19584 | tf_op jit(solution)/shard_map/reduce_sum | solution.py:35
  373.7 15.7 %all-to-all-done = f32[32,2,2,2,4,512]{5,4,3,2,1,0:T(4,128)S(1)} async-done(((f32[32,2,2,2,4,512]{5,4,3,2,1,0:T(4,128)}), f32[32,2,2,2,4,512]{5,4,3,2,1,0:T(4,128)S(1)}, u32[]{:S(2)}, u32[]{:S(2)}) %all-to-all-start) | async-done | bytes 2097184 | tf_op jit(solution)/shard_map/all_to_all | solution.py:84
  389.4 20.9 %reshape.233 = f32[8,4,2,2,2,4,64,8]{7,6,5,4,3,2,1,0:T(8,128)} reshape(f32[32,2,2,2,4,512]{5,4,3,2,1,0:T(4,128)S(1)} %all-to-all-done) | data formatting | bytes 4194304 | tf_op jit(solution)/shard_map/reshape | solution.py:85
  410.3 20.7 %copy.76 = f32[8,4,2,2,2,4,64,8]{6,0,3,7,4,5,1,2:T(8,128)} copy(f32[8,4,2,2,2,4,64,8]{7,6,5,4,3,2,1,0:T(8,128)} %reshape.233) | data formatting | bytes 4194304 | tf_op jit(solution)/shard_map/reshape | solution.py:85
  431.0 4.2 convolution_bitcast_fusion.1
  435.2 4.6 copy.107
  439.9 4.5 reshape.236
  444.4 11.2 %fusion.5 = f32[2,128,1024]{2,1,0:T(8,128)S(1)} fusion(f32[2,2,1024,1024]{3,2,0,1:T(8,128)} %all-gather.8.cloned.1.call-done, f32[2,2,1024,128]{2,3,0,1:T(8,128)S(1)} %reshape.236), kind=kOutput, calls=%fused_computation.9 | convolution fusion | flops 3221225472 | bytes 10485760 | tf_op jit(solution)/shard_map/qmk,qkn->qmn/dot_general | solution.py:15
  455.7 13.0 %fusion.17 = f32[2,1024,128]{1,2,0:T(8,128)} fusion(f32[2,128,1024]{2,1,0:T(8,128)S(1)} %fusion.5, f32[2,2,1024,1024]{3,2,0,1:T(8,128)} %all-gather.8.cloned.1.call-done, f32[2,2,1024,128]{2,3,0,1:T(8,128)S(1)} %reshape.236), kind=kOutput, calls=%fused_computation.30 | convolution fusion | flops 3221487616 | bytes 11534336 | tf_op jit(solution)/shard_map/qmk,qkn->qmn/dot_general | solution.py:15
  468.7 3.4 stack.30
  472.1 3.6 copy.81
  475.7 11.2 %fusion.4 = f32[2,128,1024]{2,1,0:T(8,128)S(1)} fusion(f32[2,2,1024,1024]{3,2,0,1:T(8,128)} %all-gather.8.cloned.1.call-done, f32[2,2,1024,128]{2,3,0,1:T(8,128)S(1)} %reshape.236), kind=kOutput, calls=%fused_computation.8 | convolution fusion | flops 3221225472 | bytes 10485760 | tf_op jit(solution)/shard_map/qmk,qkn->qmn/dot_general | solution.py:15
  487.0 13.0 %fusion.19 = f32[2,1024,128]{1,2,0:T(8,128)} fusion(f32[2,128,1024]{2,1,0:T(8,128)S(1)} %fusion.4, f32[2,2,1024,1024]{3,2,0,1:T(8,128)} %all-gather.8.cloned.1.call-done, f32[2,2,1024,128]{2,3,0,1:T(8,128)S(1)} %reshape.236), kind=kOutput, calls=%fused_computation.32 | convolution fusion | flops 3221487616 | bytes 11534336 | tf_op jit(solution)/shard_map/qmk,qkn->qmn/dot_general | solution.py:15
  500.0 2.8 stack.31
  503.5 0.9 copy-done.4
  504.4 4.4 fusion.14
  508.7 18.1 %copy.103 = f32[8,4,2,2,2,4,64,8]{7,6,5,4,3,2,1,0:T(8,128)} copy(f32[8,4,2,2,2,4,64,8]{6,0,7,4,3,5,2,1:T(8,128)} %fusion.14) | data formatting | bytes 4194304 | tf_op jit(solution)/shard_map/reshape | solution.py:109
  526.8 23.9 %reshape.234 = f32[32,2,2,2,4,512]{5,4,3,2,1,0:T(4,128)S(1)} reshape(f32[8,4,2,2,2,4,64,8]{7,6,5,4,3,2,1,0:T(8,128)} %copy.103) | data formatting | bytes 4194304 | tf_op jit(solution)/shard_map/reshape | solution.py:109
  550.7 32.2 %all_to_all.10 = f32[32,2,2,2,4,512]{5,4,3,2,1,0:T(4,128)} all-to-all(f32[32,2,2,2,4,512]{5,4,3,2,1,0:T(4,128)S(1)} %reshape.234), channel_id=1, replica_groups=mesh['kpt'=8,'row'=4,'col'=4] {'kpt','row'}, dimensions={0} | all-to-all | bytes 4194304 | tf_op jit(solution)/shard_map/all_to_all | solution.py:112
  582.9 22.5 %reshape.235 = f32[8,4,2,2,2,4,64,8]{7,6,5,4,3,2,1,0:T(8,128)} reshape(f32[32,2,2,2,4,512]{5,4,3,2,1,0:T(4,128)} %all_to_all.10) | data formatting | bytes 4194304 | tf_op jit(solution)/shard_map/reshape | solution.py:113
  605.3 19.9 %copy.86 = f32[8,4,2,2,2,4,64,8]{6,0,2,7,4,1,5,3:T(8,128)} copy(f32[8,4,2,2,2,4,64,8]{7,6,5,4,3,2,1,0:T(8,128)} %reshape.235) | data formatting | bytes 4194304 | tf_op jit(solution)/shard_map/reshape | solution.py:113
  625.2 4.1 convolution_bitcast_fusion
  629.3 4.8 copy.87
  634.1 5.3 reshape.224
  639.5 2.9 copy.88
  642.4 2.1 maximum_add_fusion
  644.5 1.5 copy.89
  (50 shorter events, 3.2 us)
Async XLA Ops:
  6.5 88.6 %all-gather.4.cloned.1.call-start = ((), (), s32[]{:S(2)}) async-start(), calls=%async_computation.2 | async-start | bytes 10485760 | tf_op jit(solution)/shard_map/all_gather | solution.py:62
  9.6 242.3 %all-gather.6.cloned.1.call-start = ((), (), s32[]{:S(2)}) async-start(), calls=%async_computation.3 | async-start | bytes 20971520 | tf_op jit(solution)/shard_map/all_gather | solution.py:64
  14.3 1.2 copy-start.5
  14.3 2.3 copy-start.6
  14.3 2.4 copy-start.7
  14.3 2.5 copy-start.8
  14.3 430.1 %all-gather.8.cloned.1.call-start = ((), (), s32[]{:S(2)}) async-start(), calls=%async_computation.4 | async-start | bytes 17825792 | tf_op jit(solution)/shard_map/all_gather | solution.py:103
  251.9 10.9 %copy-start = (f32[2,2,256,2048]{3,2,0,1:T(8,128)S(1)}, f32[2,2,256,2048]{3,2,0,1:T(8,128)}, u32[]{:S(2)}) copy-start(f32[2,2,256,2048]{3,2,0,1:T(8,128)} %all-gather.4.cloned.1.call-done) | copy-start | bytes 25165828
  276.0 12.4 %slice-start = ((s8[8388608]{0:T(1024)(128)(4,1)}), s8[4194304]{0:T(1024)(128)(4,1)S(1)}, s32[]{:S(2)}) async-start(s8[8388608]{0:T(1024)(128)(4,1)} %bitcast.121), calls=%async_computation.5 | async-start | bytes 8388608
  277.6 10.8 %slice-start.1 = ((s8[8388608]{0:T(1024)(128)(4,1)}), s8[4194304]{0:T(1024)(128)(4,1)S(1)}, s32[]{:S(2)}) async-start(s8[8388608]{0:T(1024)(128)(4,1)} %bitcast.121), calls=%async_computation.6 | async-start | bytes 8388608
  298.2 4.6 copy-start.1
  300.8 2.2 copy-start.3
  350.7 38.7 %all-to-all-start = ((f32[32,2,2,2,4,512]{5,4,3,2,1,0:T(4,128)}), f32[32,2,2,2,4,512]{5,4,3,2,1,0:T(4,128)S(1)}, u32[]{:S(2)}, u32[]{:S(2)}) async-start(f32[32,2,2,2,4,512]{5,4,3,2,1,0:T(4,128)} %reshape.232), calls=%async_computation | async-start | bytes 4194304 | tf_op jit(solution)/shard_map/all_to_all | solution.py:84
  502.8 1.6 copy-start.4
  634.1 8.3 %copy-start.2 = (f32[2,256,512]{2,1,0:T(8,128)S(1)}, f32[2,256,512]{2,1,0:T(8,128)}, u32[]{:S(2)}) copy-start(f32[2,256,512]{2,1,0:T(8,128)} %copy-done.1) | copy-start | bytes 3145732
Sparse Core Ops, SparseCore 0:
  9.8 85.3 all-gather.3
  96.8 155.0 all-gather.5
  254.1 115.8 all-gather.7
where the time goes:
time: 660 us; the launch traced here: 653 us
  waiting for transfers between devices  248 us (38%)
  local copies, waits for them, and re-layouts  225 us (34%)
  matrix products  107 us (16%)
  blocking collectives  32.2 us (5%)
  other arithmetic  19.9 us (3%)
  between operations  13.8 us (2%)
  starting transfers between devices  8 us (1%)
    all_gather x1, waiting for transfers between devices, body(): lax.all_gather(cycle_integrals, 'row', axis=2, tiled=True)  157 us
    dot_general x8, matrix products, multiply(): jnp.einsum('qmk,qkn->qmn', first_mat, second_mat, precision=PRECISE, pref...  89.7 us
    all_gather x1, waiting for transfers between devices, body(): whole_amp = lax.all_gather(cycle_amplitudes, 'col', axis=3, tiled=True)  75.1 us
    reshape x2, local copies, waits for them, and re-layouts, body(): outgoing.reshape(kpt_count * row_count, slot_count, slot_count, 2, row_kp...  43.4 us
    reshape x2, local copies, waits for them, and re-layouts, body(): returned.reshape(kpt_count, row_count, slot_count, slot_count, 2, row_kpo...  42.4 us
    reshape x2, local copies, waits for them, and re-layouts, body(): sent_back.reshape(kpt_count * row_count, slot_count, slot_count, 2, row_k...  42 us
    reshape x2, local copies, waits for them, and re-layouts, body(): incoming.reshape(kpt_count, row_count, slot_count, slot_count, 2, row_kpo...  41.5 us
    all_to_all x1, blocking collectives, body(): lax.all_to_all(sent_back, ('kpt', 'row'), split_axis=0, concat_axis=0, ti...  32.2 us
  transfers between devices with their start and end apart: 4, of which 3 were waited for; matrix products, arithmetic and copies ran while one was open for 27% of the time, Pallas kernels for 0%

commit v1 on v0

v1 whole, which is shorter than its diff:
```python
import jax
import jax.numpy as jnp
from jax import lax
from jax.experimental import pallas as pl
from jax.experimental.pallas import tpu as pltpu
from jax.sharding import PartitionSpec as P

MESH = pl.DeviceIdType.MESH
F32 = jnp.float32
BF16 = jnp.bfloat16


def split(value):
    high = value.astype(BF16)
    return high, (value - high.astype(F32)).astype(BF16)


def dot3(left, right, dims):
    def dot(a, b):
        return lax.dot_general(a, b, (dims, ((), ())), preferred_element_type=F32)

    return dot(left[0], right[0]) + (dot(left[0], right[1]) + dot(left[1], right[0]))


def exchange_kernel(
    a_in, b_in, w_in, table, transfers, momenta,
    out, out_table,
    a32, b32, w32, bh, bl, c32, ct, cg, gsend, grecv, gt, gh, gl, r32, rsend,
    tg, ts, tk, inv_t, inv_m,
    a_ys, a_yr, a_xs, a_xr, a_fs, a_fr, a_ss, a_sr,
    w_ys, w_yr, w_xs, w_xr, w_fs, w_fr, w_ss, w_sr,
    b_s, b_r, g_s, g_r, r_s, r_r,
):
    k, y, x = lax.axis_index("kpt"), lax.axis_index("row"), lax.axis_index("col")
    z, c = k // 2, lax.rem(k, 2)
    me = 4 * z + y
    left, right, far = lax.rem(x + 3, 4), lax.rem(x + 1, 4), lax.rem(x + 2, 4)
    right_dev, left_dev, twin = (k, y, right), (k, y, left), (2 * z + 1 - c, y, x)

    def rcopy(src, dst, send_sem, recv_sem, dev):
        return pltpu.make_async_remote_copy(
            src_ref=src, dst_ref=dst, send_sem=send_sem, recv_sem=recv_sem,
            device_id=dev, device_id_type=MESH,
        )

    barrier = pltpu.get_barrier_semaphore()

    def greet(at, carry):
        dk, dy = at // 4, lax.rem(at, 4)

        @pl.when(jnp.logical_or(dk != k, dy != y))
        def _():
            pl.semaphore_signal(barrier, inc=1, device_id=(dk, dy, x), device_id_type=MESH)

        return carry

    lax.fori_loop(0, 32, greet, 0)
    pl.semaphore_signal(barrier, inc=1, device_id=right_dev, device_id_type=MESH)
    pl.semaphore_signal(barrier, inc=1, device_id=left_dev, device_id_type=MESH)
    pl.semaphore_wait(barrier, 33)

    def order(n):
        return lax.rem(y + n + (n // 2) * (1 - 2 * lax.rem(n, 2)), 4)

    def row_dest(i, core):
        return (2 * z + core, 2 * c + i, x)

    def is_self(i, core):
        return jnp.logical_and(2 * c + i == y, c == core)

    def start_rows(source, dest, send, recv):
        for i in range(2):
            for core in range(2):
                own = is_self(i, core)

                @pl.when(own)
                def _():
                    pltpu.make_async_copy(source(i, core), dest(core), recv.at[y]).start()

                @pl.when(jnp.logical_not(own))
                def _():
                    rcopy(source(i, core), dest(core), send.at[2 * i + core], recv.at[y], row_dest(i, core)).start()

    def end_rows(source, dest, send, recv):
        for i in range(2):
            for core in range(2):

                @pl.when(jnp.logical_not(is_self(i, core)))
                def _():
                    rcopy(source(i, core), dest(core), send.at[2 * i + core], recv.at[y], row_dest(i, core)).wait_send()

    class Spread:
        def __init__(self, block, rows, sems):
            self.block, self.rows = block, rows
            self.ys, self.yr, self.xs, self.xr, self.fs, self.fr, self.ss, self.sr = sems

        def wait_row(self, m):
            blk = self.block(c, m, x)
            rcopy(blk, blk, self.ys.at[0], self.yr.at[m], twin).wait_recv()

        def across(self, pos, m):
            at = (x, left, right, far)[pos]
            blk = self.block(c, m, at)
            return rcopy(blk, blk, self.ss.at[pos, m], self.sr.at[pos, m], twin)

        def wait_across(self, m):
            for pos, at in enumerate((x, left, right, far)):
                blk = self.block(1 - c, m, at)
                rcopy(blk, blk, self.ss.at[pos, m], self.sr.at[pos, m], twin).wait_recv()

        def step(self, side, m):
            blk = self.block(c, m, x)
            dev = right_dev if side == 0 else left_dev
            return rcopy(blk, blk, self.xs.at[side, m], self.xr.at[side, m], dev)

        def relay(self, side, m):
            blk = self.half(m, left if side == 0 else right, side)
            dev = right_dev if side == 0 else left_dev
            return rcopy(blk, blk, self.fs.at[side, m], self.fr.at[side, m], dev)

        def half(self, m, at, side):
            return self.block(c, m, at).at[pl.ds(side * (self.rows // 2), self.rows // 2)]

        def forward_own(self, m):
            self.step(0, m).start()
            self.step(1, m).start()
            self.across(0, m).start()

        def forward_near(self, m):
            for side, at in ((0, left), (1, right)):
                blk = self.block(c, m, at)
                rcopy(blk, blk, self.xs.at[side, m], self.xr.at[side, m], twin).wait_recv()
                self.relay(side, m).start()
                self.across(1 + side, m).start()

        def forward_far(self, m):
            for side in range(2):
                blk = self.half(m, far, side)
                rcopy(blk, blk, self.fs.at[side, m], self.fr.at[side, m], twin).wait_recv()
            self.across(3, m).start()

        def end(self, m):
            for side in range(2):
                self.step(side, m).wait_send()
                self.relay(side, m).wait_send()
            for pos in range(4):
                self.across(pos, m).wait_send()

    spread_a = Spread(
        lambda core, m, at: a32.at[core, m, at], 256, (a_ys, a_yr, a_xs, a_xr, a_fs, a_fr, a_ss, a_sr)
    )
    spread_w = Spread(
        lambda core, m, at: w32.at[core, 4 * m + at], 64, (w_ys, w_yr, w_xs, w_xr, w_fs, w_fr, w_ss, w_sr)
    )

    a_rows = (lambda i, core: a_in.at[i, core], lambda core: a32.at[core, y, x], a_ys, a_yr)
    w_rows = (lambda i, core: w_in.at[i, core], lambda core: w32.at[core, 4 * y + x], w_ys, w_yr)
    b_rows = (
        lambda i, core: b_in.at[i, :, :, pl.ds(256 * core, 256)], lambda core: b32.at[y], b_s, b_r,
    )
    start_rows(*a_rows)
    spread_a.wait_row(y)
    spread_a.forward_own(y)

    def add(first, second):
        return table[16 * first + second, 0]

    def sub(first, second):
        return table[16 * first, second]

    def invert(label, carry):
        at_t, at_m = 0, 0
        for slot in range(16):
            at_t = jnp.where(transfers[slot] == label, slot, at_t)
            at_m = jnp.where(momenta[slot] == label, slot, at_m)
        inv_t[label] = at_t
        inv_m[label] = at_m
        return carry

    lax.fori_loop(0, 16, invert, 0)
    own_transfer, own_momentum = transfers[me], momenta[me]

    def fill(ki, carry):
        def one(at, inner):
            tg[ki, at] = sub(sub(momenta[at], own_transfer), ki)
            tk[ki, at] = sub(sub(own_momentum, transfers[at]), ki)
            ts[ki, at] = inv_t[sub(sub(own_momentum, ki), at)]
            return inner

        return lax.fori_loop(0, 16, one, carry)

    lax.fori_loop(0, 16, fill, 0)

    def fill_out(at, carry):
        total = add(transfers[2 * k + at // 4], 4 * y + lax.rem(at, 4))

        def one(kb, inner):
            out_table[at, kb] = inv_m[add(total, kb)]
            return inner

        return lax.fori_loop(0, 16, one, carry)

    lax.fori_loop(0, 8, fill_out, 0)

    for n in range(1, 4):
        spread_a.wait_row(order(n))
        spread_a.forward_own(order(n))
    end_rows(*a_rows)
    start_rows(*b_rows)
    for n in range(4):
        spread_a.forward_near(order(n))
    end_rows(*b_rows)
    start_rows(*w_rows)

    for n in range(4):
        at = order(n)
        rcopy(b32.at[at], b32.at[at], b_s.at[0], b_r.at[at], twin).wait_recv()

        def split_b(ri, carry):
            bh[at, ri], bl[at, ri] = split(b32[at, ri])
            return carry

        lax.fori_loop(0, 2, split_b, 0)

    for n in range(4):
        spread_a.forward_far(order(n))

    lower = lax.broadcasted_iota(jnp.int32, (16, 128), 1) < 64

    def pick(load, first, second):
        return jnp.where(lower, load(first), load(second))

    def g_copy(m, slot, source):
        return rcopy(
            gsend.at[m, slot], grecv.at[m, source], g_s.at[m, slot], g_r.at[m, source],
            (2 * (slot // 4) + c, lax.rem(slot, 4), x),
        )

    NN = ((1,), (0,))
    NT = ((1,), (1,))

    def cycle_block(n, carry):
        m = order(n)
        spread_a.wait_across(m)
        c32[...] = jnp.zeros_like(c32)

        def chunk(at, inner):
            a_real, a_imag = split(a32[0, m, at]), split(a32[1, m, at])
            b_real, b_imag = (bh[at, 0], bl[at, 0]), (bh[at, 1], bl[at, 1])
            c32[0] += dot3(a_real, b_real, NN) - dot3(a_imag, b_imag, NN)
            c32[1] += dot3(a_real, b_imag, NN) + dot3(a_imag, b_real, NN)
            return inner

        lax.fori_loop(0, 4, chunk, 0)
        for ri in range(2):
            for h in range(2):
                ct[ri, h] = c32[ri, 128 * h : 128 * h + 128, :].T
                for kb in range(16):
                    cg[ri, kb, :, 128 * h : 128 * h + 128] = ct[ri, h, pl.ds(kb, 16, stride=16), :]

        def to_slot(slot, inner):
            for h in range(2):
                first, second = tg[4 * m + 2 * h, slot], tg[4 * m + 2 * h + 1, slot]
                for ri in range(2):
                    gsend[m, slot, ri, :, 128 * h : 128 * h + 128] = pick(
                        lambda kb: cg[ri, kb, :, pl.ds(128 * h, 128)], first, second
                    )

            @pl.when(slot == me)
            def _():
                pltpu.make_async_copy(gsend.at[m, slot], grecv.at[m, me], g_r.at[m, me]).start()

            @pl.when(slot != me)
            def _():
                g_copy(m, slot, me).start()

            return inner

        lax.fori_loop(0, 16, to_slot, 0)

        @pl.when(n == 1)
        def _():
            for at in range(4):
                spread_w.wait_row(order(at))
                spread_w.forward_own(order(at))

        return carry

    lax.fori_loop(0, 4, cycle_block, 0)

    for n in range(4):
        spread_w.forward_near(order(n))

    def arrive(at, carry):
        slot = at // 4
        g_copy(lax.rem(at, 4), slot, slot).wait_recv()
        return carry

    lax.fori_loop(0, 64, arrive, 0)

    def gather_block(n, carry):
        m = order(n)

        def from_slot(kb, inner):
            for h in range(2):
                first, second = ts[4 * m + 2 * h, kb], ts[4 * m + 2 * h + 1, kb]
                for ri in range(2):
                    gt[ri, m, kb, :, 128 * h : 128 * h + 128] = pick(
                        lambda slot: grecv[m, slot, ri, :, pl.ds(128 * h, 128)], first, second
                    )
            return inner

        lax.fori_loop(0, 16, from_slot, 0)
        for ri in range(2):
            gh[ri, m], gl[ri, m] = split(gt[ri, m].reshape(256, 256))
        return carry

    lax.fori_loop(0, 4, gather_block, 0)

    for n in range(4):
        spread_w.forward_far(order(n))

    def r_copy(m, dest, source):
        return rcopy(rsend.at[m, dest], out.at[source], r_s.at[m, dest], r_r.at[source], (dest, m, x))

    def ladder_block(n, carry):
        m = order(n)
        spread_w.wait_across(m)
        c32[...] = jnp.zeros_like(c32)

        def chunk(at, inner):
            cols = pl.ds(pl.multiple_of(256 * at, 256), 256)
            w_real = split(w32[0, pl.ds(4 * m, 4), :, cols].reshape(256, 256))
            w_imag = split(w32[1, pl.ds(4 * m, 4), :, cols].reshape(256, 256))
            g_real, g_imag = (gh[0, at], gl[0, at]), (gh[1, at], gl[1, at])
            c32[0] += dot3(g_real, w_real, NT) - dot3(g_imag, w_imag, NT)
            c32[1] += dot3(g_imag, w_real, NT) + dot3(g_real, w_imag, NT)
            return inner

        lax.fori_loop(0, 4, chunk, 0)
        for ri in range(2):
            r32[ri] = gt[ri, m] + c32[ri].reshape(16, 16, 256)

        def to_dest(dest, inner):
            for i in range(2):
                for h in range(2):
                    first = tk[4 * m + 2 * h, 2 * dest + i]
                    second = tk[4 * m + 2 * h + 1, 2 * dest + i]
                    for ri in range(2):
                        rsend[m, dest, i, ri, :, 128 * h : 128 * h + 128] = pick(
                            lambda kb: r32[ri, kb, :, pl.ds(128 * h, 128)], first, second
                        )
            own = jnp.logical_and(dest == k, m == y)

            @pl.when(own)
            def _():
                pltpu.make_async_copy(rsend.at[m, dest], out.at[2 * me + c], r_r.at[2 * me + c]).start()

            @pl.when(jnp.logical_not(own))
            def _():
                r_copy(m, dest, 2 * me + c).start()

            return inner

        lax.fori_loop(0, 8, to_dest, 0)
        return carry

    lax.fori_loop(0, 4, ladder_block, 0)

    end_rows(*w_rows)

    def end_block(m, carry):
        spread_a.end(m)
        spread_w.end(m)

        def end_slot(slot, inner):
            @pl.when(slot != me)
            def _():
                g_copy(m, slot, me).wait_send()

            return inner

        lax.fori_loop(0, 16, end_slot, 0)

        def end_dest(dest, inner):
            @pl.when(jnp.logical_or(dest != k, m != y))
            def _():
                r_copy(m, dest, 2 * me + c).wait_send()

            return inner

        return lax.fori_loop(0, 8, end_dest, carry)

    lax.fori_loop(0, 4, end_block, 0)

    def end_source(source, carry):
        r_copy(0, 0, source).wait_recv()
        return carry

    lax.fori_loop(0, 32, end_source, 0)


def place_kernel(slot_of, parts, out, rows):
    at = 4 * pl.program_id(0)
    lower = lax.broadcasted_iota(jnp.int32, (16, 128), 1) < 64
    for h in range(2):

        def one(kb, carry):
            first, second = slot_of[at + 2 * h, kb], slot_of[at + 2 * h + 1, kb]
            for core in range(2):
                value = jnp.where(
                    lower,
                    parts[2 * first + core, 0, 0, :, pl.ds(128 * h, 128)],
                    parts[2 * second + core, 0, 0, :, pl.ds(128 * h, 128)],
                )
                rows[h, pl.ds(256 * core + kb, 16, stride=16), :] = value
            return carry

        lax.fori_loop(0, 16, one, 0)
        out[0, 0, 128 * h : 128 * h + 128, :] = rows[h].T


def body(amplitudes, integrals, weight, table, transfers, momenta):
    dma = pltpu.SemaphoreType.DMA
    spread_sems = [dma((4,)), dma((4,)), dma((2, 4)), dma((2, 4)), dma((2, 4)), dma((2, 4)), dma((4, 4)), dma((4, 4))]
    parts, slot_of = pl.pallas_call(
        exchange_kernel,
        out_shape=(
            jax.ShapeDtypeStruct((32, 2, 2, 16, 256), F32),
            jax.ShapeDtypeStruct((8, 16), jnp.int32),
        ),
        in_specs=[pl.BlockSpec(memory_space=pl.ANY)] * 3 + [pl.BlockSpec(memory_space=pltpu.SMEM)] * 3,
        out_specs=(pl.BlockSpec(memory_space=pl.ANY), pl.BlockSpec(memory_space=pltpu.SMEM)),
        scratch_shapes=[
            pltpu.VMEM((2, 4, 4, 256, 512), F32),
            pltpu.VMEM((4, 2, 512, 256), F32),
            pltpu.VMEM((2, 16, 64, 1024), F32),
            pltpu.VMEM((4, 2, 512, 256), BF16),
            pltpu.VMEM((4, 2, 512, 256), BF16),
            pltpu.VMEM((2, 256, 256), F32),
            pltpu.VMEM((2, 2, 256, 128), F32),
            pltpu.VMEM((2, 16, 16, 256), F32),
            pltpu.VMEM((4, 16, 2, 16, 256), F32),
            pltpu.VMEM((4, 16, 2, 16, 256), F32),
            pltpu.VMEM((2, 4, 16, 16, 256), F32),
            pltpu.VMEM((2, 4, 256, 256), BF16),
            pltpu.VMEM((2, 4, 256, 256), BF16),
            pltpu.VMEM((2, 16, 16, 256), F32),
            pltpu.VMEM((4, 8, 2, 2, 16, 256), F32),
            pltpu.SMEM((16, 16), jnp.int32),
            pltpu.SMEM((16, 16), jnp.int32),
            pltpu.SMEM((16, 16), jnp.int32),
            pltpu.SMEM((16,), jnp.int32),
            pltpu.SMEM((16,), jnp.int32),
        ]
        + spread_sems
        + spread_sems
        + [dma((4,)), dma((4,)), dma((4, 16)), dma((4, 16)), dma((4, 8)), dma((32,))],
        compiler_params=pltpu.CompilerParams(
            collective_id=0, has_side_effects=True, vmem_limit_bytes=60 * 2**20
        ),
        name="exchange",
    )(amplitudes, integrals, weight, table.reshape(256, 16), transfers, momenta)
    return pl.pallas_call(
        place_kernel,
        grid=(2, 2),
        out_shape=jax.ShapeDtypeStruct((2, 2, 256, 512), F32),
        in_specs=[
            pl.BlockSpec(memory_space=pltpu.SMEM),
            pl.BlockSpec((32, 1, 1, 16, 256), lambda i, ri: (0, i, ri, 0, 0)),
        ],
        out_specs=pl.BlockSpec((1, 1, 256, 512), lambda i, ri: (i, ri, 0, 0)),
        scratch_shapes=[pltpu.VMEM((2, 512, 128), F32)],
        name="place",
    )(slot_of, parts)


def solution(mesh):
    return jax.shard_map(
        body,
        mesh=mesh,
        in_specs=(
            P("kpt", None, "row", "col"),
            P("kpt", None, "row", "col"),
            P("kpt", None, ("row", "col"), None),
            P(),
            P(),
            P(),
        ),
        out_specs=P("kpt", None, "row", "col"),
        check_vma=False,
    )
```

time: 660 us -> 175 us (0.27)
  waiting for transfers between devices: 248 us -> 0 us
  local copies, waits for them, and re-layouts: 225 us -> 0 us
  Pallas kernels: 0 us -> 172 us
  matrix products: 107 us -> 0 us
  blocking collectives: 32.2 us -> 0 us
  other arithmetic: 19.9 us -> 0 us
  between operations: 13.8 us -> 0.01 us
  starting transfers between devices: 8 us -> 0 us
    all_gather x3 -> x0, waiting for transfers between devices: 232 us -> none  [the longest x1 157 us: body(): lax.all_gather(cycle_integrals, 'row', axis=2, tiled=True)]
    reshape x12 -> x0, local copies, waits for them, and re-layouts: 187 us -> none  [the longest x2 43.4 us: body(): outgoing.reshape(kpt_count * row_count, slot_count, slot_count, 2, row_kp...]
    pallas_call x0 -> x2, Pallas kernels: none -> 172 us  [the longest x1 166 us: body(): pl.pallas_call(exchange_kernel, out_shape=(jax.ShapeDtypeStruct((32, 2, 2...]
    dot_general x12 -> x0, matrix products: 107 us -> none  [the longest x8 89.7 us: multiply(): jnp.einsum('qmk,qkn->qmn', first_mat, second_mat, precision=PRECISE, pref...]
    all_to_all x1 -> x0, blocking collectives: 32.2 us -> none  [body(): lax.all_to_all(sent_back, ('kpt', 'row'), split_axis=0, concat_axis=0, ti...]
    another operation x8 -> x0, local copies, waits for them, and re-layouts: 18.5 us -> none  [complex_product(): return jnp.stack([real_part, imag_part], axis=1)]
    reduce_sum x4 -> x0, other arithmetic: 17.1 us -> none  [table_lookup(): jnp.sum(one_first[..., :, None] * one_second[..., None, :] * lookup_table...]
    all_to_all x1 -> x0, waiting for transfers between devices: 15.7 us -> none  [body(): lax.all_to_all(outgoing, ('kpt', 'row'), split_axis=0, concat_axis=0, til...]
  transfers between devices with their start and end apart: 4 -> 0, of which waited for: 3 -> 0; matrix products, arithmetic and copies ran while one was open for 27% -> 0% of each run, Pallas kernels for 0% -> 0%
where the time goes in v1:
time: 175 us; the launch traced here: 172 us
  Pallas kernels  172 us (98%)
    pallas_call x1, Pallas kernels, body(): pl.pallas_call(exchange_kernel, out_shape=(jax.ShapeDtypeStruct((32, 2, 2...  166 us
    pallas_call x1, Pallas kernels, body(): pl.pallas_call(place_kernel, grid=(2, 2), out_shape=jax.ShapeDtypeStruct(...  5.38 us

profile of v1, /device:TPU:9, one launch (start us, length us, event | category | flops | bytes accessed | tf_op | source)
XLA Modules:
  0.0 171.9 jit_solution(4563152166224463567)
XLA Ops:
  0.0 166.5 %exchange.1 = (f32[32,2,2,16,256]{4,3,2,1,0:T(8,128)}, s32[8,16]{1,0:T(8,128)}) custom-call(f32[2,2,256,512]{3,2,1,0:T(8,128)} %a_in.1, f32[2,2,512,512]{3,2,1,0:T(8,128)} %b_in.1, f32[2,2,64,1024]{3,2,1,0:T(8,128)} %w_in.1, s32[256,16]{1,0:T(8,128)} %bitcast.1, s32[16]{0:T(128)} %transfers.1, s32[16]{0:T(128)} %momenta.1), custom_call_target="tpu_custom_call" | custom-call | tf_op jit(solution)/shard_map/exchange/pallas_call | solution.py:426
  166.5 5.4 %place.1 = f32[2,2,256,512]{3,2,1,0:T(8,128)} custom-call(s32[8,16]{1,0:T(8,128)} %get-tuple-element.7.slot_of, f32[32,2,2,16,256]{4,3,2,1,0:T(8,128)} %get-tuple-element.8.parts), custom_call_target="tpu_custom_call" | custom-call | tf_op jit(solution)/shard_map/place/pallas_call | solution.py:464

commit v2 on v1

--- a/solution.py
+++ b/solution.py
@@ -23,10 +23,10 @@
 
 
 def exchange_kernel(
-    a_in, b_in, w_in, table, transfers, momenta,
+    a_in, b_in, w_in, table_in, transfers_in, momenta_in,
     out, out_table,
     a32, b32, w32, bh, bl, c32, ct, cg, gsend, grecv, gt, gh, gl, r32, rsend,
-    tg, ts, tk, inv_t, inv_m,
+    table, transfers, momenta, tg, ts, tk, inv_t, inv_m, table_sem,
     a_ys, a_yr, a_xs, a_xr, a_fs, a_fr, a_ss, a_sr,
     w_ys, w_yr, w_xs, w_xr, w_fs, w_fr, w_ss, w_sr,
     b_s, b_r, g_s, g_r, r_s, r_r,
@@ -45,16 +45,11 @@
 
     barrier = pltpu.get_barrier_semaphore()
 
-    def greet(at, carry):
-        dk, dy = at // 4, lax.rem(at, 4)
-
-        @pl.when(jnp.logical_or(dk != k, dy != y))
-        def _():
-            pl.semaphore_signal(barrier, inc=1, device_id=(dk, dy, x), device_id_type=MESH)
-
-        return carry
-
-    lax.fori_loop(0, 32, greet, 0)
+    for step in range(1, 32):
+        dk = 2 * lax.rem(z + step // 8, 4) + lax.rem(c + step // 4 % 2, 2)
+        pl.semaphore_signal(
+            barrier, inc=1, device_id=(dk, lax.rem(y + step % 4, 4), x), device_id_type=MESH
+        )
     pl.semaphore_signal(barrier, inc=1, device_id=right_dev, device_id_type=MESH)
     pl.semaphore_signal(barrier, inc=1, device_id=left_dev, device_id_type=MESH)
     pl.semaphore_wait(barrier, 33)
@@ -62,32 +57,55 @@
     def order(n):
         return lax.rem(y + n + (n // 2) * (1 - 2 * lax.rem(n, 2)), 4)
 
-    def row_dest(i, core):
-        return (2 * z + core, 2 * c + i, x)
-
-    def is_self(i, core):
-        return jnp.logical_and(2 * c + i == y, c == core)
-
-    def start_rows(source, dest, send, recv):
-        for i in range(2):
+    def far_order(n):
+        return lax.rem(y + 2 + 3 * n, 4)
+
+    near_i, other_i = 1 - lax.rem(y, 2), lax.rem(y, 2)
+    home = c == y // 2
+
+    class Rows:
+        def __init__(self, source, dest, send, recv):
+            self.source, self.dest, self.send, self.recv = source, dest, send, recv
+
+        def copy(self, near, core):
+            i = near_i if near else other_i
+            return rcopy(
+                self.source(i, core), self.dest(core), self.send.at[core if near else 2 + core],
+                self.recv.at[y], (2 * z + core, 2 * c + i, x),
+            )
+
+        def start_near(self):
             for core in range(2):
-                own = is_self(i, core)
-
-                @pl.when(own)
+                self.copy(True, core).start()
+
+        def start_home(self):
+            for core in range(2):
+
+                @pl.when(jnp.logical_and(home, c == core))
                 def _():
-                    pltpu.make_async_copy(source(i, core), dest(core), recv.at[y]).start()
-
-                @pl.when(jnp.logical_not(own))
+                    pltpu.make_async_copy(self.source(other_i, core), self.dest(core), self.recv.at[y]).start()
+
+                @pl.when(jnp.logical_and(home, c != core))
                 def _():
-                    rcopy(source(i, core), dest(core), send.at[2 * i + core], recv.at[y], row_dest(i, core)).start()
-
-    def end_rows(source, dest, send, recv):
-        for i in range(2):
+                    self.copy(False, core).start()
+
+        def start_far(self):
             for core in range(2):
 
-                @pl.when(jnp.logical_not(is_self(i, core)))
+                @pl.when(jnp.logical_not(home))
                 def _():
-                    rcopy(source(i, core), dest(core), send.at[2 * i + core], recv.at[y], row_dest(i, core)).wait_send()
+                    self.copy(False, core).start()
+
+        def end_near(self):
+            for core in range(2):
+                self.copy(True, core).wait_send()
+
+        def end_other(self):
+            for core in range(2):
+
+                @pl.when(jnp.logical_not(jnp.logical_and(home, c == core)))
+                def _():
+                    self.copy(False, core).wait_send()
 
     class Spread:
         def __init__(self, block, rows, sems):
@@ -153,14 +171,30 @@
         lambda core, m, at: w32.at[core, 4 * m + at], 64, (w_ys, w_yr, w_xs, w_xr, w_fs, w_fr, w_ss, w_sr)
     )
 
-    a_rows = (lambda i, core: a_in.at[i, core], lambda core: a32.at[core, y, x], a_ys, a_yr)
-    w_rows = (lambda i, core: w_in.at[i, core], lambda core: w32.at[core, 4 * y + x], w_ys, w_yr)
-    b_rows = (
-        lambda i, core: b_in.at[i, :, :, pl.ds(256 * core, 256)], lambda core: b32.at[y], b_s, b_r,
-    )
-    start_rows(*a_rows)
+    a_rows = Rows(lambda i, core: a_in.at[i, core], lambda core: a32.at[core, y, x], a_ys, a_yr)
+    w_rows = Rows(lambda i, core: w_in.at[i, core], lambda core: w32.at[core, 4 * y + x], w_ys, w_yr)
+    b_rows = Rows(lambda i, core: b_in.at[i, :, :, pl.ds(256 * core, 256)], lambda core: b32.at[y], b_s, b_r)
+    for rows in (a_rows, b_rows, w_rows):
+        rows.start_home()
+    a_rows.start_near()
+    a_rows.start_far()
+    b_rows.start_near()
+    w_rows.start_near()
+    w_rows.start_far()
+    b_rows.start_far()
     spread_a.wait_row(y)
     spread_a.forward_own(y)
+
+    tables = [
+        pltpu.make_async_copy(source, dest, table_sem.at[at])
+        for at, (source, dest) in enumerate(
+            ((table_in, table), (transfers_in, transfers), (momenta_in, momenta))
+        )
+    ]
+    for copy in tables:
+        copy.start()
+    for copy in tables:
+        copy.wait()
 
     def add(first, second):
         return table[16 * first + second, 0]
@@ -202,28 +236,58 @@
 
     lax.fori_loop(0, 8, fill_out, 0)
 
-    for n in range(1, 4):
+    def split_b(n):
+        at = order(n)
+        rcopy(b32.at[at], b32.at[at], b_s.at[0], b_r.at[at], twin).wait_recv()
+
+        def one(ri, carry):
+            bh[at, ri], bl[at, ri] = split(b32[at, ri])
+            return carry
+
+        lax.fori_loop(0, 2, one, 0)
+
+    NN = ((1,), (0,))
+    NT = ((1,), (1,))
+
+    def cycle_chunk(m, at):
+        a_real, a_imag = split(a32[0, m, at]), split(a32[1, m, at])
+        b_real, b_imag = (bh[at, 0], bl[at, 0]), (bh[at, 1], bl[at, 1])
+        c32[m, 0] += dot3(a_real, b_real, NN) - dot3(a_imag, b_imag, NN)
+        c32[m, 1] += dot3(a_real, b_imag, NN) + dot3(a_imag, b_real, NN)
+
+    def early_chunks(n):
+        m = order(n)
+        spread_a.wait_across(m)
+
+        def one(at, carry):
+            cycle_chunk(m, order(at))
+            return carry
+
+        lax.fori_loop(0, 3, one, 0)
+
+    c32[...] = jnp.zeros_like(c32)
+    for n in (1, 2, 3):
         spread_a.wait_row(order(n))
         spread_a.forward_own(order(n))
-    end_rows(*a_rows)
-    start_rows(*b_rows)
+        if n < 3:
+            spread_a.forward_near(order(n - 1))
+    split_b(0)
+    spread_a.forward_far(y)
+    spread_a.forward_near(order(2))
+    split_b(1)
+    split_b(2)
+    early_chunks(0)
+    spread_a.forward_far(order(1))
+    early_chunks(1)
+    spread_a.forward_near(order(3))
     for n in range(4):
-        spread_a.forward_near(order(n))
-    end_rows(*b_rows)
-    start_rows(*w_rows)
-
-    for n in range(4):
-        at = order(n)
-        rcopy(b32.at[at], b32.at[at], b_s.at[0], b_r.at[at], twin).wait_recv()
-
-        def split_b(ri, carry):
-            bh[at, ri], bl[at, ri] = split(b32[at, ri])
-            return carry
-
-        lax.fori_loop(0, 2, split_b, 0)
-
-    for n in range(4):
-        spread_a.forward_far(order(n))
+        spread_w.wait_row(far_order(n))
+        spread_w.forward_own(far_order(n))
+    spread_a.forward_far(order(2))
+    early_chunks(2)
+    spread_a.forward_far(order(3))
+    early_chunks(3)
+    split_b(3)
 
     lower = lax.broadcasted_iota(jnp.int32, (16, 128), 1) < 64
 
@@ -236,29 +300,18 @@
             (2 * (slot // 4) + c, lax.rem(slot, 4), x),
         )
 
-    NN = ((1,), (0,))
-    NT = ((1,), (1,))
-
     def cycle_block(n, carry):
         m = order(n)
-        spread_a.wait_across(m)
-        c32[...] = jnp.zeros_like(c32)
-
-        def chunk(at, inner):
-            a_real, a_imag = split(a32[0, m, at]), split(a32[1, m, at])
-            b_real, b_imag = (bh[at, 0], bl[at, 0]), (bh[at, 1], bl[at, 1])
-            c32[0] += dot3(a_real, b_real, NN) - dot3(a_imag, b_imag, NN)
-            c32[1] += dot3(a_real, b_imag, NN) + dot3(a_imag, b_real, NN)
-            return inner
-
-        lax.fori_loop(0, 4, chunk, 0)
+        cycle_chunk(m, order(3))
         for ri in range(2):
             for h in range(2):
-                ct[ri, h] = c32[ri, 128 * h : 128 * h + 128, :].T
+                ct[ri, h] = c32[m, ri, 128 * h : 128 * h + 128, :].T
                 for kb in range(16):
                     cg[ri, kb, :, 128 * h : 128 * h + 128] = ct[ri, h, pl.ds(kb, 16, stride=16), :]
 
-        def to_slot(slot, inner):
+        def to_slot(step, inner):
+            slot_z, slot_y = lax.rem(z + 2 + 3 * (step // 4), 4), lax.rem(y + 2 + 3 * lax.rem(step, 4), 4)
+            slot = 4 * slot_z + slot_y
             for h in range(2):
                 first, second = tg[4 * m + 2 * h, slot], tg[4 * m + 2 * h + 1, slot]
                 for ri in range(2):
@@ -277,19 +330,13 @@
             return inner
 
         lax.fori_loop(0, 16, to_slot, 0)
-
-        @pl.when(n == 1)
-        def _():
-            for at in range(4):
-                spread_w.wait_row(order(at))
-                spread_w.forward_own(order(at))
-
         return carry
 
     lax.fori_loop(0, 4, cycle_block, 0)
-
     for n in range(4):
-        spread_w.forward_near(order(n))
+        spread_w.forward_near(far_order(n))
+    for n in (0, 1):
+        spread_w.forward_far(far_order(n))
 
     def arrive(at, carry):
         slot = at // 4
@@ -317,31 +364,34 @@
 
     lax.fori_loop(0, 4, gather_block, 0)
 
-    for n in range(4):
-        spread_w.forward_far(order(n))
-
     def r_copy(m, dest, source):
         return rcopy(rsend.at[m, dest], out.at[source], r_s.at[m, dest], r_r.at[source], (dest, m, x))
 
     def ladder_block(n, carry):
-        m = order(n)
+        m = far_order(n)
+
+        @pl.when(n < 2)
+        def _():
+            spread_w.forward_far(far_order(n + 2))
+
         spread_w.wait_across(m)
-        c32[...] = jnp.zeros_like(c32)
+        c32[0] = jnp.zeros_like(c32[0])
 
         def chunk(at, inner):
             cols = pl.ds(pl.multiple_of(256 * at, 256), 256)
             w_real = split(w32[0, pl.ds(4 * m, 4), :, cols].reshape(256, 256))
             w_imag = split(w32[1, pl.ds(4 * m, 4), :, cols].reshape(256, 256))
             g_real, g_imag = (gh[0, at], gl[0, at]), (gh[1, at], gl[1, at])
-            c32[0] += dot3(g_real, w_real, NT) - dot3(g_imag, w_imag, NT)
-            c32[1] += dot3(g_imag, w_real, NT) + dot3(g_real, w_imag, NT)
+            c32[0, 0] += dot3(g_real, w_real, NT) - dot3(g_imag, w_imag, NT)
+            c32[0, 1] += dot3(g_imag, w_real, NT) + dot3(g_real, w_imag, NT)
             return inner
 
         lax.fori_loop(0, 4, chunk, 0)
         for ri in range(2):
-            r32[ri] = gt[ri, m] + c32[ri].reshape(16, 16, 256)
-
-        def to_dest(dest, inner):
+            r32[ri] = gt[ri, m] + c32[0, ri].reshape(16, 16, 256)
+
+        def to_dest(step, inner):
+            dest = 2 * lax.rem(z + 2 + 3 * (step // 2), 4) + lax.rem(step, 2)
             for i in range(2):
                 for h in range(2):
                     first = tk[4 * m + 2 * h, 2 * dest + i]
@@ -367,7 +417,9 @@
 
     lax.fori_loop(0, 4, ladder_block, 0)
 
-    end_rows(*w_rows)
+    for rows in (a_rows, b_rows, w_rows):
+        rows.end_near()
+        rows.end_other()
 
     def end_block(m, carry):
         spread_a.end(m)
@@ -416,7 +468,7 @@
                 rows[h, pl.ds(256 * core + kb, 16, stride=16), :] = value
             return carry
 
-        lax.fori_loop(0, 16, one, 0)
+        lax.fori_loop(0, 16, one, 0, unroll=True)
         out[0, 0, 128 * h : 128 * h + 128, :] = rows[h].T
 
 
@@ -429,7 +481,7 @@
             jax.ShapeDtypeStruct((32, 2, 2, 16, 256), F32),
             jax.ShapeDtypeStruct((8, 16), jnp.int32),
         ),
-        in_specs=[pl.BlockSpec(memory_space=pl.ANY)] * 3 + [pl.BlockSpec(memory_space=pltpu.SMEM)] * 3,
+        in_specs=[pl.BlockSpec(memory_space=pl.ANY)] * 6,
         out_specs=(pl.BlockSpec(memory_space=pl.ANY), pl.BlockSpec(memory_space=pltpu.SMEM)),
         scratch_shapes=[
             pltpu.VMEM((2, 4, 4, 256, 512), F32),
@@ -437,7 +489,7 @@
             pltpu.VMEM((2, 16, 64, 1024), F32),
             pltpu.VMEM((4, 2, 512, 256), BF16),
             pltpu.VMEM((4, 2, 512, 256), BF16),
-            pltpu.VMEM((2, 256, 256), F32),
+            pltpu.VMEM((4, 2, 256, 256), F32),
             pltpu.VMEM((2, 2, 256, 128), F32),
             pltpu.VMEM((2, 16, 16, 256), F32),
             pltpu.VMEM((4, 16, 2, 16, 256), F32),
@@ -447,11 +499,15 @@
             pltpu.VMEM((2, 4, 256, 256), BF16),
             pltpu.VMEM((2, 16, 16, 256), F32),
             pltpu.VMEM((4, 8, 2, 2, 16, 256), F32),
+            pltpu.SMEM((256, 16), jnp.int32),
+            pltpu.SMEM((16,), jnp.int32),
+            pltpu.SMEM((16,), jnp.int32),
             pltpu.SMEM((16, 16), jnp.int32),
             pltpu.SMEM((16, 16), jnp.int32),
             pltpu.SMEM((16, 16), jnp.int32),
             pltpu.SMEM((16,), jnp.int32),
             pltpu.SMEM((16,), jnp.int32),
+            dma((3,)),
         ]
         + spread_sems
         + spread_sems

time: 175 us -> 169 us (0.966); the launches traced: 172 us -> 169 us
  Pallas kernels: 172 us -> 169 us
    pallas_call x1, Pallas kernels: 166 us -> 164 us  [body(): pl.pallas_call(exchange_kernel, out_shape=(jax.ShapeDtypeStruct((32, 2, 2...]
where the time goes in v2:
time: 169 us
  Pallas kernels  169 us (100%)
    pallas_call x1, Pallas kernels, body(): pl.pallas_call(exchange_kernel, out_shape=(jax.ShapeDtypeStruct((32, 2, 2...  164 us
    pallas_call x1, Pallas kernels, body(): pl.pallas_call(place_kernel, grid=(2, 2), out_shape=jax.ShapeDtypeStruct(...  4.5 us

profile of v2, /device:TPU:9, one launch (start us, length us, event | category | flops | bytes accessed | tf_op | source)
XLA Modules:
  0.0 168.8 jit_solution(10814193736250631272)
XLA Ops:
  0.0 164.3 %exchange.1 = (f32[32,2,2,16,256]{4,3,2,1,0:T(8,128)}, s32[8,16]{1,0:T(8,128)}) custom-call(f32[2,2,256,512]{3,2,1,0:T(8,128)} %a_in.1, f32[2,2,512,512]{3,2,1,0:T(8,128)} %b_in.1, f32[2,2,64,1024]{3,2,1,0:T(8,128)} %w_in.1, s32[256,16]{1,0:T(8,128)} %bitcast.1, s32[16]{0:T(128)} %transfers_in.1, s32[16]{0:T(128)} %momenta_in.1), custom_call_target="tpu_custom_call" | custom-call | tf_op jit(solution)/shard_map/exchange/pallas_call | solution.py:478
  164.3 4.5 %place.1 = f32[2,2,256,512]{3,2,1,0:T(8,128)} custom-call(s32[8,16]{1,0:T(8,128)} %get-tuple-element.7.slot_of, f32[32,2,2,16,256]{4,3,2,1,0:T(8,128)} %get-tuple-element.8.parts), custom_call_target="tpu_custom_call" | custom-call | tf_op jit(solution)/shard_map/place/pallas_call | solution.py:520

commit v3 on v2

--- a/solution.py
+++ b/solution.py
@@ -274,18 +274,18 @@
     split_b(0)
     spread_a.forward_far(y)
     spread_a.forward_near(order(2))
+    spread_a.forward_far(order(1))
+    spread_a.forward_near(order(3))
     split_b(1)
     split_b(2)
     early_chunks(0)
-    spread_a.forward_far(order(1))
+    spread_a.forward_far(order(2))
     early_chunks(1)
-    spread_a.forward_near(order(3))
+    spread_a.forward_far(order(3))
     for n in range(4):
         spread_w.wait_row(far_order(n))
         spread_w.forward_own(far_order(n))
-    spread_a.forward_far(order(2))
     early_chunks(2)
-    spread_a.forward_far(order(3))
     early_chunks(3)
     split_b(3)
 

time: 169 us -> 154 us (0.911)
  Pallas kernels: 169 us -> 152 us
    pallas_call x1, Pallas kernels: 164 us -> 148 us  [body(): pl.pallas_call(exchange_kernel, out_shape=(jax.ShapeDtypeStruct((32, 2, 2...]
where the time goes in v3:
time: 154 us; the launch traced here: 152 us
  Pallas kernels  152 us (99%)
    pallas_call x1, Pallas kernels, body(): pl.pallas_call(exchange_kernel, out_shape=(jax.ShapeDtypeStruct((32, 2, 2...  148 us
    pallas_call x1, Pallas kernels, body(): pl.pallas_call(place_kernel, grid=(2, 2), out_shape=jax.ShapeDtypeStruct(...  4.5 us

profile of v3, /device:TPU:9, one launch (start us, length us, event | category | flops | bytes accessed | tf_op | source)
XLA Modules:
  0.0 152.5 jit_solution(12343984719074955815)
XLA Ops:
  0.0 148.0 %exchange.1 = (f32[32,2,2,16,256]{4,3,2,1,0:T(8,128)}, s32[8,16]{1,0:T(8,128)}) custom-call(f32[2,2,256,512]{3,2,1,0:T(8,128)} %a_in.1, f32[2,2,512,512]{3,2,1,0:T(8,128)} %b_in.1, f32[2,2,64,1024]{3,2,1,0:T(8,128)} %w_in.1, s32[256,16]{1,0:T(8,128)} %bitcast.1, s32[16]{0:T(128)} %transfers_in.1, s32[16]{0:T(128)} %momenta_in.1), custom_call_target="tpu_custom_call" | custom-call | tf_op jit(solution)/shard_map/exchange/pallas_call | solution.py:478
  148.0 4.5 %place.1 = f32[2,2,256,512]{3,2,1,0:T(8,128)} custom-call(s32[8,16]{1,0:T(8,128)} %get-tuple-element.7.slot_of, f32[32,2,2,16,256]{4,3,2,1,0:T(8,128)} %get-tuple-element.8.parts), custom_call_target="tpu_custom_call" | custom-call | tf_op jit(solution)/shard_map/place/pallas_call | solution.py:520

commit v4 on v3

--- a/solution.py
+++ b/solution.py
@@ -52,13 +52,22 @@
         )
     pl.semaphore_signal(barrier, inc=1, device_id=right_dev, device_id_type=MESH)
     pl.semaphore_signal(barrier, inc=1, device_id=left_dev, device_id_type=MESH)
+    tables = [
+        pltpu.make_async_copy(source, dest, table_sem.at[at])
+        for at, (source, dest) in enumerate(
+            ((table_in, table), (transfers_in, transfers), (momenta_in, momenta))
+        )
+    ]
+    for copy in tables:
+        copy.start()
+    c32[...] = jnp.zeros_like(c32)
     pl.semaphore_wait(barrier, 33)
 
     def order(n):
         return lax.rem(y + n + (n // 2) * (1 - 2 * lax.rem(n, 2)), 4)
 
     def far_order(n):
-        return lax.rem(y + 2 + 3 * n, 4)
+        return lax.rem(y + 2 + 3 * n + (n // 2) * (3 - 2 * lax.rem(n, 2)), 4)
 
     near_i, other_i = 1 - lax.rem(y, 2), lax.rem(y, 2)
     home = c == y // 2
@@ -185,14 +194,6 @@
     spread_a.wait_row(y)
     spread_a.forward_own(y)
 
-    tables = [
-        pltpu.make_async_copy(source, dest, table_sem.at[at])
-        for at, (source, dest) in enumerate(
-            ((table_in, table), (transfers_in, transfers), (momenta_in, momenta))
-        )
-    ]
-    for copy in tables:
-        copy.start()
     for copy in tables:
         copy.wait()
 
@@ -265,7 +266,6 @@
 
         lax.fori_loop(0, 3, one, 0)
 
-    c32[...] = jnp.zeros_like(c32)
     for n in (1, 2, 3):
         spread_a.wait_row(order(n))
         spread_a.forward_own(order(n))
@@ -456,20 +456,19 @@
     at = 4 * pl.program_id(0)
     lower = lax.broadcasted_iota(jnp.int32, (16, 128), 1) < 64
     for h in range(2):
-
-        def one(kb, carry):
+        for kb in range(16):
             first, second = slot_of[at + 2 * h, kb], slot_of[at + 2 * h + 1, kb]
-            for core in range(2):
-                value = jnp.where(
-                    lower,
-                    parts[2 * first + core, 0, 0, :, pl.ds(128 * h, 128)],
-                    parts[2 * second + core, 0, 0, :, pl.ds(128 * h, 128)],
-                )
-                rows[h, pl.ds(256 * core + kb, 16, stride=16), :] = value
-            return carry
-
-        lax.fori_loop(0, 16, one, 0, unroll=True)
-        out[0, 0, 128 * h : 128 * h + 128, :] = rows[h].T
+            for ri in range(2):
+                for core in range(2):
+                    value = jnp.where(
+                        lower,
+                        parts[2 * first + core, 0, ri, :, pl.ds(128 * h, 128)],
+                        parts[2 * second + core, 0, ri, :, pl.ds(128 * h, 128)],
+                    )
+                    rows[ri, h, pl.ds(256 * core + kb, 16, stride=16), :] = value
+    for ri in range(2):
+        for h in range(2):
+            out[0, ri, 128 * h : 128 * h + 128, :] = rows[ri, h].T
 
 
 def body(amplitudes, integrals, weight, table, transfers, momenta):
@@ -519,14 +518,14 @@
     )(amplitudes, integrals, weight, table.reshape(256, 16), transfers, momenta)
     return pl.pallas_call(
         place_kernel,
-        grid=(2, 2),
+        grid=(2,),
         out_shape=jax.ShapeDtypeStruct((2, 2, 256, 512), F32),
         in_specs=[
             pl.BlockSpec(memory_space=pltpu.SMEM),
-            pl.BlockSpec((32, 1, 1, 16, 256), lambda i, ri: (0, i, ri, 0, 0)),
+            pl.BlockSpec((32, 1, 2, 16, 256), lambda i: (0, i, 0, 0, 0)),
         ],
-        out_specs=pl.BlockSpec((1, 1, 256, 512), lambda i, ri: (i, ri, 0, 0)),
-        scratch_shapes=[pltpu.VMEM((2, 512, 128), F32)],
+        out_specs=pl.BlockSpec((1, 2, 256, 512), lambda i: (i, 0, 0, 0)),
+        scratch_shapes=[pltpu.VMEM((2, 2, 512, 128), F32)],
         name="place",
     )(slot_of, parts)
 

time: 154 us -> 154 us (level)
  no operation moved by 1% of the time
where the time goes in v4:
time: 154 us; the launch traced here: 152 us
  Pallas kernels  152 us (99%)
    pallas_call x1, Pallas kernels, body(): pl.pallas_call(exchange_kernel, out_shape=(jax.ShapeDtypeStruct((32, 2, 2...  149 us
    pallas_call x1, Pallas kernels, body(): pl.pallas_call(place_kernel, grid=(2,), out_shape=jax.ShapeDtypeStruct((2...  3.4 us

profile of v4, /device:TPU:9, one launch (start us, length us, event | category | flops | bytes accessed | tf_op | source)
XLA Modules:
  0.0 152.5 jit_solution(13350696622426432248)
XLA Ops:
  0.0 149.1 %exchange.1 = (f32[32,2,2,16,256]{4,3,2,1,0:T(8,128)}, s32[8,16]{1,0:T(8,128)}) custom-call(f32[2,2,256,512]{3,2,1,0:T(8,128)} %a_in.1, f32[2,2,512,512]{3,2,1,0:T(8,128)} %b_in.1, f32[2,2,64,1024]{3,2,1,0:T(8,128)} %w_in.1, s32[256,16]{1,0:T(8,128)} %bitcast.1, s32[16]{0:T(128)} %transfers_in.1, s32[16]{0:T(128)} %momenta_in.1), custom_call_target="tpu_custom_call" | custom-call | tf_op jit(solution)/shard_map/exchange/pallas_call | solution.py:477
  149.1 3.4 %place.1 = f32[2,2,256,512]{3,2,1,0:T(8,128)} custom-call(s32[8,16]{1,0:T(8,128)} %get-tuple-element.7.slot_of, f32[32,2,2,16,256]{4,3,2,1,0:T(8,128)} %get-tuple-element.8.parts), custom_call_target="tpu_custom_call" | custom-call | tf_op jit(solution)/shard_map/place/pallas_call | solution.py:519

commit v5 on v4

--- a/solution.py
+++ b/solution.py
@@ -52,22 +52,13 @@
         )
     pl.semaphore_signal(barrier, inc=1, device_id=right_dev, device_id_type=MESH)
     pl.semaphore_signal(barrier, inc=1, device_id=left_dev, device_id_type=MESH)
-    tables = [
-        pltpu.make_async_copy(source, dest, table_sem.at[at])
-        for at, (source, dest) in enumerate(
-            ((table_in, table), (transfers_in, transfers), (momenta_in, momenta))
-        )
-    ]
-    for copy in tables:
-        copy.start()
-    c32[...] = jnp.zeros_like(c32)
     pl.semaphore_wait(barrier, 33)
 
     def order(n):
         return lax.rem(y + n + (n // 2) * (1 - 2 * lax.rem(n, 2)), 4)
 
     def far_order(n):
-        return lax.rem(y + 2 + 3 * n + (n // 2) * (3 - 2 * lax.rem(n, 2)), 4)
+        return lax.rem(y + 2 + 3 * n, 4)
 
     near_i, other_i = 1 - lax.rem(y, 2), lax.rem(y, 2)
     home = c == y // 2
@@ -194,6 +185,14 @@
     spread_a.wait_row(y)
     spread_a.forward_own(y)
 
+    tables = [
+        pltpu.make_async_copy(source, dest, table_sem.at[at])
+        for at, (source, dest) in enumerate(
+            ((table_in, table), (transfers_in, transfers), (momenta_in, momenta))
+        )
+    ]
+    for copy in tables:
+        copy.start()
     for copy in tables:
         copy.wait()
 
@@ -266,6 +265,7 @@
 
         lax.fori_loop(0, 3, one, 0)
 
+    c32[...] = jnp.zeros_like(c32)
     for n in (1, 2, 3):
         spread_a.wait_row(order(n))
         spread_a.forward_own(order(n))

time: 154 us -> 153 us (level)
  no operation moved by 1% of the time
where the time goes in v5:
time: 153 us; the launch traced here: 151 us
  Pallas kernels  151 us (99%)
    pallas_call x1, Pallas kernels, body(): pl.pallas_call(exchange_kernel, out_shape=(jax.ShapeDtypeStruct((32, 2, 2...  148 us
    pallas_call x1, Pallas kernels, body(): pl.pallas_call(place_kernel, grid=(2,), out_shape=jax.ShapeDtypeStruct((2...  3.4 us

profile of v5, /device:TPU:9, one launch (start us, length us, event | category | flops | bytes accessed | tf_op | source)
XLA Modules:
  0.0 151.4 jit_solution(16322502167056515014)
XLA Ops:
  0.0 148.0 %exchange.1 = (f32[32,2,2,16,256]{4,3,2,1,0:T(8,128)}, s32[8,16]{1,0:T(8,128)}) custom-call(f32[2,2,256,512]{3,2,1,0:T(8,128)} %a_in.1, f32[2,2,512,512]{3,2,1,0:T(8,128)} %b_in.1, f32[2,2,64,1024]{3,2,1,0:T(8,128)} %w_in.1, s32[256,16]{1,0:T(8,128)} %bitcast.1, s32[16]{0:T(128)} %transfers_in.1, s32[16]{0:T(128)} %momenta_in.1), custom_call_target="tpu_custom_call" | custom-call | tf_op jit(solution)/shard_map/exchange/pallas_call | solution.py:477
  148.0 3.4 %place.1 = f32[2,2,256,512]{3,2,1,0:T(8,128)} custom-call(s32[8,16]{1,0:T(8,128)} %get-tuple-element.7.slot_of, f32[32,2,2,16,256]{4,3,2,1,0:T(8,128)} %get-tuple-element.8.parts), custom_call_target="tpu_custom_call" | custom-call | tf_op jit(solution)/shard_map/place/pallas_call | solution.py:519
